TPU v7x, 32 devices: a whole 2x2x4 slice. The times are simulated.
32 devices in a mesh: chan: 4 (over z), seg: 4 (over x, core), lag: 2 (over y).
Axes of the slice: x: 2, y: 2, z: 4, core: 2. Of those that a mesh axis runs over, the one named last changes fastest.
Arguments:
- spectra: bfloat16 [4, 2500, 2, 6144], P('seg', 'chan', None, 'lag'), may hold values from -6 to 6
- pair_local: int32 [4, 3, 256], replicated, may hold values from 0 to 624
- pair_partner: int32 [4, 3, 256], replicated, may hold values from 0 to 624, as said below
- pair_bin: int32 [4, 3, 256], replicated, may hold values from 0 to 1
- pair_owner: int32 [4, 3, 256], replicated, may hold values 0 or 1
- pair_count: int32 [4, 3], replicated, may hold values from 64 to 256, as said below
Outputs:
- stacks: float32 [2500, 2, 2048], P('chan', None, 'lag')
Inputs may be any that keep to these rules, and one draw needn't show every extreme that they name: `pair_partner`: in round 0 the two channels of a pair differ. `pair_count`: some block reaches 256 in some round.
All inputs are finite; a program needn't handle non-finite values.
Results may differ from a plain program's by a relative error of at most 0.0065.
Values may be sent and summed in bfloat16 or wider, within the bound.
A program may use at most 128 MiB of HBM per device.

v0:
```python
import math

import jax
import jax.numpy as jnp
from jax import lax
from jax.sharding import PartitionSpec as P

FREQ = 6144
LAGS = 2048
ROUNDS = 3
BINS = 2


def shifted(block, axis, distance):
    devices = range(lax.axis_size(axis))
    route = [((i - distance) % len(devices), i) for i in devices]
    return lax.ppermute(block, axis, route)


def one_hot_rows(target_rows, mask_rows, total_rows):
    row_ids = jnp.arange(total_rows, dtype=jnp.int32)[:, None]
    return ((row_ids == target_rows[None, :]) & mask_rows[None, :]).astype(jnp.float32)


def bin_rows(selector, corr):
    return lax.dot_general(
        selector,
        corr,
        (((1,), (1,)), ((), ())),
        precision=lax.Precision.HIGHEST,
        preferred_element_type=jnp.float32,
    )


def per_device(spectra, pair_local, pair_partner, pair_bin, pair_owner, pair_count):
    block_index = lax.axis_index("chan")
    lag_index = lax.axis_index("lag")
    own_block = spectra[0]
    block_chans = own_block.shape[0]
    half_freq = own_block.shape[2]
    half_lags = LAGS // lax.axis_size("lag")
    total_rows = block_chans * BINS
    slot_count = pair_local.shape[2]
    freq_index = lag_index * half_freq + jnp.arange(half_freq, dtype=jnp.int32) + 1
    corr_scale = FREQ ** (-0.5)
    slot_ids = jnp.arange(slot_count, dtype=jnp.int32)
    local_stack = jnp.zeros((total_rows, half_lags), jnp.float32)
    for round_index in range(ROUNDS):
        first_index = pair_local[block_index, round_index]
        second_index = pair_partner[block_index, round_index]
        first = jnp.take(own_block, first_index, axis=0).astype(jnp.float32)
        if round_index == 0:
            second = jnp.take(own_block, second_index, axis=0).astype(jnp.float32)
        else:
            partner_block = shifted(own_block, "chan", -round_index)
            second = jnp.take(partner_block, second_index, axis=0).astype(jnp.float32)
        cross_real = first[:, 0] * second[:, 0] + first[:, 1] * second[:, 1]
        cross_imag = first[:, 1] * second[:, 0] - first[:, 0] * second[:, 1]
        cross = jnp.concatenate([cross_real, cross_imag], axis=1).astype(jnp.bfloat16)
        block_rows = math.gcd(lax.axis_size("lag") * half_lags, 512)

        def one_block(offset):
            taus = offset + jnp.arange(block_rows, dtype=jnp.int32) - LAGS // 2
            phase = jnp.mod(taus[:, None] * freq_index[None, :], 2 * FREQ)
            angle = phase.astype(jnp.float32) * (math.pi / FREQ)
            table = jnp.concatenate([jnp.cos(angle), -jnp.sin(angle)], axis=1).astype(jnp.bfloat16)
            return (
                lax.dot_general(
                    table, cross, (((1,), (1,)), ((), ())), preferred_element_type=jnp.float32
                )
                * corr_scale
            )

        offsets = (
            jnp.arange(lax.axis_size("lag") * half_lags // block_rows, dtype=jnp.int32) * block_rows
        )
        corr = lax.psum_scatter(
            lax.map(one_block, offsets).reshape(lax.axis_size("lag") * half_lags, slot_count),
            "lag",
            scatter_dimension=0,
            tiled=True,
        )
        live = slot_ids < pair_count[block_index, round_index]
        owners = pair_owner[block_index, round_index]
        bins_now = pair_bin[block_index, round_index]
        own_rows = jnp.where(owners == 0, first_index, second_index) * BINS + bins_now
        if round_index == 0:
            local_stack = bin_rows(one_hot_rows(own_rows, live, total_rows), corr)
        else:
            mine_rows = first_index * BINS + bins_now
            local_stack = local_stack + bin_rows(
                one_hot_rows(mine_rows, live & (owners == 0), total_rows), corr
            )
            partner_rows = second_index * BINS + bins_now
            partner_stack = bin_rows(
                one_hot_rows(partner_rows, live & (owners == 1), total_rows), corr
            )
            local_stack = local_stack + shifted(partner_stack, "chan", round_index)
    local_stack = lax.psum(local_stack, "seg")
    return local_stack.reshape(block_chans, BINS, half_lags)


def solution(mesh):
    return jax.shard_map(
        per_device,
        mesh=mesh,
        in_specs=(P("seg", "chan", None, "lag"), P(), P(), P(), P(), P()),
        out_specs=P("chan", None, "lag"),
        check_vma=False,
    )
```

profile of v0, /device:TPU:0, one launch (start us, length us, event | category | flops | bytes accessed | tf_op | source)
XLA Modules:
  0.0 1158.6 jit_solution(11971192236451308695)
XLA Ops:
  48.8 16.5 %gather_fusion.1 = bf16[256,2,3072]{2,1,0:T(2,128)(2,1)} fusion(bf16[625,2,3072]{2,1,0:T(2,128)(2,1)} %bitcast.83, s32[1024]{0:T(1024)S(1)} %get-tuple-element.327), kind=kCustom, calls=%fused_computation.1.clone | custom fusion | bytes 6292480 | tf_op jit(solution)/shard_map/jit(_take)/gather | solution.py:53
  65.8 16.6 %gather_fusion.4 = bf16[256,2,3072]{2,1,0:T(2,128)(2,1)} fusion(bf16[625,2,3072]{2,1,0:T(2,128)(2,1)} %bitcast.84, s32[1024]{0:T(1024)S(1)} %pad_clamp_fusion.1), kind=kCustom, calls=%fused_computation.4.clone | custom fusion | bytes 6292480 | tf_op jit(solution)/shard_map/jit(_take)/gather | solution.py:51
  99.2 78.4 %collective-permute-done = bf16[625,2,3072]{2,1,0:T(2,128)(2,1)} collective-permute-done((bf16[625,2,3072]{2,1,0:T(2,128)(2,1)}, bf16[625,2,3072]{2,1,0:T(2,128)(2,1)}, u32[]{:S(2)}, u32[]{:S(2)}) %collective-permute-start) | collective-permute-done | bytes 7680032 | tf_op jit(solution)/shard_map/ppermute | solution.py:17
  177.6 16.5 %gather_fusion.3 = bf16[256,2,3072]{2,1,0:T(2,128)(2,1)} fusion(bf16[625,2,3072]{2,1,0:T(2,128)(2,1)} %collective-permute-done, s32[1024]{0:T(1024)S(1)} %pad_clamp_fusion.2), kind=kCustom, calls=%fused_computation.3.clone | custom fusion | bytes 6292480 | tf_op jit(solution)/shard_map/jit(_take)/gather | solution.py:56
  217.1 118.2 %while.40 = (s32[]{:T(128)}, f32[4,512,256]{2,1,0:T(8,128)S(1)}, s32[4]{0:T(128)S(1)}, bf16[256,6144]{1,0:T(8,128)(2,1)}, s32[]{:T(128)}, /*index=5*/s32[]{:T(128)}) while((s32[]{:T(128)}, f32[4,512,256]{2,1,0:T(8,128)S(1)}, s32[4]{0:T(128)S(1)}, bf16[256,6144]{1,0:T(8,128)(2,1)}, s32[]{:T(128)}, /*index=5*/s32[]{:T(128)}) %tuple.118), condition=%wide.region_4.6_spmd.clone, body=%wide.region_3.5_spmd.clone.sunk | while | flops 1642208256 | bytes 28864632 | solution.py:78
  218.4 26.3 %cosine_convert_fusion.7 = (bf16[512,3072]{1,0:T(8,128)(2,1)S(1)}, bf16[512,3072]{1,0:T(8,128)(2,1)S(1)}) fusion(s32[3072]{0:T(1024)S(1)} %add_add_fusion.15, s32[512]{0:T(512)S(1)} %add_add_fusion.16), kind=kLoop, calls=%fused_computation.36.clone.1 | loop fusion | flops 18874368 | bytes 6305792 | tf_op jit(solution)/shard_map/convert.2
  248.0 26.3 %cosine_convert_fusion.7 = (bf16[512,3072]{1,0:T(8,128)(2,1)S(1)}, bf16[512,3072]{1,0:T(8,128)(2,1)S(1)}) fusion(s32[3072]{0:T(1024)S(1)} %add_add_fusion.15, s32[512]{0:T(512)S(1)} %add_add_fusion.16), kind=kLoop, calls=%fused_computation.36.clone.1 | loop fusion | flops 18874368 | bytes 6305792 | tf_op jit(solution)/shard_map/convert.2
  277.6 26.3 %cosine_convert_fusion.7 = (bf16[512,3072]{1,0:T(8,128)(2,1)S(1)}, bf16[512,3072]{1,0:T(8,128)(2,1)S(1)}) fusion(s32[3072]{0:T(1024)S(1)} %add_add_fusion.15, s32[512]{0:T(512)S(1)} %add_add_fusion.16), kind=kLoop, calls=%fused_computation.36.clone.1 | loop fusion | flops 18874368 | bytes 6305792 | tf_op jit(solution)/shard_map/convert.2
  307.1 26.3 %cosine_convert_fusion.7 = (bf16[512,3072]{1,0:T(8,128)(2,1)S(1)}, bf16[512,3072]{1,0:T(8,128)(2,1)S(1)}) fusion(s32[3072]{0:T(1024)S(1)} %add_add_fusion.15, s32[512]{0:T(512)S(1)} %add_add_fusion.16), kind=kLoop, calls=%fused_computation.36.clone.1 | loop fusion | flops 18874368 | bytes 6305792 | tf_op jit(solution)/shard_map/convert.2
  336.8 168.7 %collective-permute-done.2 = bf16[625,2,3072]{2,1,0:T(2,128)(2,1)} collective-permute-done((bf16[625,2,3072]{2,1,0:T(2,128)(2,1)}, bf16[625,2,3072]{2,1,0:T(2,128)(2,1)}, u32[]{:S(2)}, u32[]{:S(2)}) %collective-permute-start.2) | collective-permute-done | bytes 7680032 | tf_op jit(solution)/shard_map/ppermute | solution.py:17
  505.5 16.9 %gather_fusion.5 = bf16[256,2,3072]{2,1,0:T(2,128)(2,1)} fusion(bf16[625,2,3072]{2,1,0:T(2,128)(2,1)} %collective-permute-done.2, s32[1024]{0:T(1024)S(1)} %pad_clamp_fusion), kind=kCustom, calls=%fused_computation.5.clone | custom fusion | bytes 6292480 | tf_op jit(solution)/shard_map/jit(_take)/gather | solution.py:56
  546.8 121.2 %while.41 = (s32[]{:T(128)}, f32[4,512,256]{2,1,0:T(8,128)}, s32[4]{0:T(128)S(1)}, bf16[256,6144]{1,0:T(8,128)(2,1)}, s32[]{:T(128)}, /*index=5*/s32[]{:T(128)}) while((s32[]{:T(128)}, f32[4,512,256]{2,1,0:T(8,128)}, s32[4]{0:T(128)S(1)}, bf16[256,6144]{1,0:T(8,128)(2,1)}, s32[]{:T(128)}, /*index=5*/s32[]{:T(128)}) %tuple.132), condition=%wide.region_7.9_spmd.clone, body=%wide.region_6.8_spmd.clone.sunk | while | flops 1642208256 | bytes 28865140 | solution.py:78
  548.4 26.3 %cosine_convert_fusion.8 = (bf16[512,3072]{1,0:T(8,128)(2,1)S(1)}, bf16[512,3072]{1,0:T(8,128)(2,1)S(1)}) fusion(s32[3072]{0:T(1024)S(1)} %add_add_fusion.17, s32[512]{0:T(512)S(1)} %add_add_fusion.18), kind=kLoop, calls=%fused_computation.55.clone.1 | loop fusion | flops 18874368 | bytes 6305792 | tf_op jit(solution)/shard_map/convert.4
  578.6 26.3 %cosine_convert_fusion.8 = (bf16[512,3072]{1,0:T(8,128)(2,1)S(1)}, bf16[512,3072]{1,0:T(8,128)(2,1)S(1)}) fusion(s32[3072]{0:T(1024)S(1)} %add_add_fusion.17, s32[512]{0:T(512)S(1)} %add_add_fusion.18), kind=kLoop, calls=%fused_computation.55.clone.1 | loop fusion | flops 18874368 | bytes 6305792 | tf_op jit(solution)/shard_map/convert.4
  608.8 26.3 %cosine_convert_fusion.8 = (bf16[512,3072]{1,0:T(8,128)(2,1)S(1)}, bf16[512,3072]{1,0:T(8,128)(2,1)S(1)}) fusion(s32[3072]{0:T(1024)S(1)} %add_add_fusion.17, s32[512]{0:T(512)S(1)} %add_add_fusion.18), kind=kLoop, calls=%fused_computation.55.clone.1 | loop fusion | flops 18874368 | bytes 6305792 | tf_op jit(solution)/shard_map/convert.4
  639.0 26.3 %cosine_convert_fusion.8 = (bf16[512,3072]{1,0:T(8,128)(2,1)S(1)}, bf16[512,3072]{1,0:T(8,128)(2,1)S(1)}) fusion(s32[3072]{0:T(1024)S(1)} %add_add_fusion.17, s32[512]{0:T(512)S(1)} %add_add_fusion.18), kind=kLoop, calls=%fused_computation.55.clone.1 | loop fusion | flops 18874368 | bytes 6305792 | tf_op jit(solution)/shard_map/convert.4
  709.6 117.7 %while.39 = (s32[]{:T(128)}, f32[4,512,256]{2,1,0:T(8,128)S(1)}, s32[4]{0:T(128)S(1)}, bf16[256,6144]{1,0:T(8,128)(2,1)}, s32[]{:T(128)}, /*index=5*/s32[]{:T(128)}) while((s32[]{:T(128)}, f32[4,512,256]{2,1,0:T(8,128)S(1)}, s32[4]{0:T(128)S(1)}, bf16[256,6144]{1,0:T(8,128)(2,1)}, s32[]{:T(128)}, /*index=5*/s32[]{:T(128)}) %tuple.133), condition=%wide.region_1.3_spmd.clone, body=%wide.region_0.0_spmd.clone.sunk | while | flops 1642208256 | bytes 28864632 | solution.py:78
  710.9 26.3 %cosine_convert_fusion.6 = (bf16[512,3072]{1,0:T(8,128)(2,1)S(1)}, bf16[512,3072]{1,0:T(8,128)(2,1)S(1)}) fusion(s32[3072]{0:T(1024)S(1)} %add_add_fusion.13, s32[512]{0:T(512)S(1)} %add_add_fusion.14), kind=kLoop, calls=%fused_computation.17.clone.1 | loop fusion | flops 18874368 | bytes 6305792 | tf_op jit(solution)/shard_map/convert
  740.3 26.3 %cosine_convert_fusion.6 = (bf16[512,3072]{1,0:T(8,128)(2,1)S(1)}, bf16[512,3072]{1,0:T(8,128)(2,1)S(1)}) fusion(s32[3072]{0:T(1024)S(1)} %add_add_fusion.13, s32[512]{0:T(512)S(1)} %add_add_fusion.14), kind=kLoop, calls=%fused_computation.17.clone.1 | loop fusion | flops 18874368 | bytes 6305792 | tf_op jit(solution)/shard_map/convert
  769.7 26.3 %cosine_convert_fusion.6 = (bf16[512,3072]{1,0:T(8,128)(2,1)S(1)}, bf16[512,3072]{1,0:T(8,128)(2,1)S(1)}) fusion(s32[3072]{0:T(1024)S(1)} %add_add_fusion.13, s32[512]{0:T(512)S(1)} %add_add_fusion.14), kind=kLoop, calls=%fused_computation.17.clone.1 | loop fusion | flops 18874368 | bytes 6305792 | tf_op jit(solution)/shard_map/convert
  799.2 26.3 %cosine_convert_fusion.6 = (bf16[512,3072]{1,0:T(8,128)(2,1)S(1)}, bf16[512,3072]{1,0:T(8,128)(2,1)S(1)}) fusion(s32[3072]{0:T(1024)S(1)} %add_add_fusion.13, s32[512]{0:T(512)S(1)} %add_add_fusion.14), kind=kLoop, calls=%fused_computation.17.clone.1 | loop fusion | flops 18874368 | bytes 6305792 | tf_op jit(solution)/shard_map/convert
  830.9 28.0 %reduce-scatter.4.cloned.1.call-done = f32[1024,256]{1,0:T(8,128)} async-done(((f32[2048,256]{1,0:T(8,128)}), f32[1024,256]{1,0:T(8,128)}) %reduce-scatter.4.cloned.1.call-update) | async-done | bytes 1048592 | tf_op jit(solution)/shard_map/reduce_scatter | solution.py:77
  864.7 164.4 %collective-permute-done.3 = f32[1250,1024]{1,0:T(8,128)} collective-permute-done((f32[1250,1024]{1,0:T(8,128)}, f32[1250,1024]{1,0:T(8,128)}, u32[]{:S(2)}, u32[]{:S(2)}) %collective-permute-start.3) | collective-permute-done | bytes 5120032 | tf_op jit(solution)/shard_map/ppermute | solution.py:17
  1045.9 99.2 %all-reduce.2.cloned.1.call-done = f32[625,2,1024]{2,1,0:T(2,128)} async-done(((f32[625,2,1024]{2,1,0:T(2,128)}), f32[625,2,1024]{2,1,0:T(2,128)}) %all-reduce.2.cloned.1.call-update) | async-done | bytes 5120016 | tf_op jit(solution)/shard_map/psum | solution.py:99
  (174 shorter events, 222.8 us)
Async XLA Ops:
  6.5 681.8 %reduce-scatter.6.cloned.1.call-start = ((), (), s32[]{:S(2)}) async-start(), calls=%async_computation.4 | async-start | bytes 3145728 | tf_op jit(solution)/shard_map/reduce_scatter | solution.py:77
  6.5 171.0 %collective-permute-start = (bf16[625,2,3072]{2,1,0:T(2,128)(2,1)}, bf16[625,2,3072]{2,1,0:T(2,128)(2,1)}, u32[]{:S(2)}, u32[]{:S(2)}) collective-permute-start(bf16[625,2,3072]{2,1,0:T(2,128)(2,1)} %bitcast.79), channel_id=1, source_target_pairs={{8,0},{16,8},{24,16},{0,24},{9,1},{17,9},{25,17},{1,25},{10,2},{18... | collective-permute-start | bytes 23040008 | tf_op jit(solution)/shard_map/ppermute | solution.py:17
  11.6 493.9 %collective-permute-start.2 = (bf16[625,2,3072]{2,1,0:T(2,128)(2,1)}, bf16[625,2,3072]{2,1,0:T(2,128)(2,1)}, u32[]{:S(2)}, u32[]{:S(2)}) collective-permute-start(bf16[625,2,3072]{2,1,0:T(2,128)(2,1)} %bitcast.80), channel_id=1, source_target_pairs={{16,0},{24,8},{0,16},{8,24},{17,1},{25,9},{1,17},{9,25},{18,2},{26... | collective-permute-start | bytes 23040008 | tf_op jit(solution)/shard_map/ppermute | solution.py:17
  218.4 26.3 %copy-start.8 = (bf16[256,6144]{1,0:T(8,128)(2,1)S(1)}, bf16[256,6144]{1,0:T(8,128)(2,1)}, u32[]{:S(2)}) copy-start(bf16[256,6144]{1,0:T(8,128)(2,1)} %get-tuple-element.467) | copy-start | bytes 9437188 | tf_op jit(solution)/shard_map/while
  248.0 26.3 %copy-start.8 = (bf16[256,6144]{1,0:T(8,128)(2,1)S(1)}, bf16[256,6144]{1,0:T(8,128)(2,1)}, u32[]{:S(2)}) copy-start(bf16[256,6144]{1,0:T(8,128)(2,1)} %get-tuple-element.467) | copy-start | bytes 9437188 | tf_op jit(solution)/shard_map/while
  277.5 26.3 %copy-start.8 = (bf16[256,6144]{1,0:T(8,128)(2,1)S(1)}, bf16[256,6144]{1,0:T(8,128)(2,1)}, u32[]{:S(2)}) copy-start(bf16[256,6144]{1,0:T(8,128)(2,1)} %get-tuple-element.467) | copy-start | bytes 9437188 | tf_op jit(solution)/shard_map/while
  307.1 26.3 %copy-start.8 = (bf16[256,6144]{1,0:T(8,128)(2,1)S(1)}, bf16[256,6144]{1,0:T(8,128)(2,1)}, u32[]{:S(2)}) copy-start(bf16[256,6144]{1,0:T(8,128)(2,1)} %get-tuple-element.467) | copy-start | bytes 9437188 | tf_op jit(solution)/shard_map/while
  336.8 364.5 %reduce-scatter.8.cloned.1.call-start = ((), (), s32[]{:S(2)}) async-start(), calls=%async_computation.5 | async-start | bytes 3145728 | tf_op jit(solution)/shard_map/reduce_scatter | solution.py:77
  546.8 121.3 %copy-start = (bf16[256,2,3072]{2,1,0:T(2,128)(2,1)S(1)}, bf16[256,2,3072]{2,1,0:T(2,128)(2,1)}, u32[]{:S(2)}) copy-start(bf16[256,2,3072]{2,1,0:T(2,128)(2,1)} %gather_fusion.1) | copy-start | bytes 9437188
  548.4 26.3 %copy-start.9 = (bf16[256,6144]{1,0:T(8,128)(2,1)S(1)}, bf16[256,6144]{1,0:T(8,128)(2,1)}, u32[]{:S(2)}) copy-start(bf16[256,6144]{1,0:T(8,128)(2,1)} %get-tuple-element.449) | copy-start | bytes 9437188 | tf_op jit(solution)/shard_map/while
  578.6 26.3 %copy-start.9 = (bf16[256,6144]{1,0:T(8,128)(2,1)S(1)}, bf16[256,6144]{1,0:T(8,128)(2,1)}, u32[]{:S(2)}) copy-start(bf16[256,6144]{1,0:T(8,128)(2,1)} %get-tuple-element.449) | copy-start | bytes 9437188 | tf_op jit(solution)/shard_map/while
  608.8 26.3 %copy-start.9 = (bf16[256,6144]{1,0:T(8,128)(2,1)S(1)}, bf16[256,6144]{1,0:T(8,128)(2,1)}, u32[]{:S(2)}) copy-start(bf16[256,6144]{1,0:T(8,128)(2,1)} %get-tuple-element.449) | copy-start | bytes 9437188 | tf_op jit(solution)/shard_map/while
  639.0 26.3 %copy-start.9 = (bf16[256,6144]{1,0:T(8,128)(2,1)S(1)}, bf16[256,6144]{1,0:T(8,128)(2,1)}, u32[]{:S(2)}) copy-start(bf16[256,6144]{1,0:T(8,128)(2,1)} %get-tuple-element.449) | copy-start | bytes 9437188 | tf_op jit(solution)/shard_map/while
  668.0 190.8 %reduce-scatter.4.cloned.1.call-start = ((), (), s32[]{:S(2)}) async-start(), calls=%async_computation.3 | async-start | bytes 3145728 | tf_op jit(solution)/shard_map/reduce_scatter | solution.py:77
  694.2 170.5 %collective-permute-start.1 = (f32[1250,1024]{1,0:T(8,128)}, f32[1250,1024]{1,0:T(8,128)}, u32[]{:S(2)}, u32[]{:S(2)}) collective-permute-start(f32[1250,1024]{1,0:T(8,128)} %fusion.75), channel_id=1, source_target_pairs={{24,0},{0,8},{8,16},{16,24},{25,1},{1,9},{9,17},{17,25},{26,2},{2,... | collective-permute-start | bytes 15360008 | tf_op jit(solution)/shard_map/ppermute | solution.py:17
  707.0 322.2 %collective-permute-start.3 = (f32[1250,1024]{1,0:T(8,128)}, f32[1250,1024]{1,0:T(8,128)}, u32[]{:S(2)}, u32[]{:S(2)}) collective-permute-start(f32[1250,1024]{1,0:T(8,128)} %fusion.81), channel_id=1, source_target_pairs={{16,0},{24,8},{0,16},{8,24},{17,1},{25,9},{1,17},{9,25},{18,2},{26... | collective-permute-start | bytes 15360008 | tf_op jit(solution)/shard_map/ppermute | solution.py:17
  709.6 120.0 %copy-start.13 = (pred[256]{0:T(512)(128)(4,1)S(1)}, pred[256]{0:T(512)(128)(4,1)}, u32[]{:S(2)}) copy-start(pred[256]{0:T(512)(128)(4,1)} %get-tuple-element.249) | copy-start | bytes 772
  709.6 120.0 %copy-start.14 = (pred[256]{0:T(512)(128)(4,1)S(1)}, pred[256]{0:T(512)(128)(4,1)}, u32[]{:S(2)}) copy-start(pred[256]{0:T(512)(128)(4,1)} %get-tuple-element.253) | copy-start | bytes 772
  709.6 149.3 %copy-start.11 = (s32[256]{0:T(256)S(1)}, s32[256]{0:T(256)}, u32[]{:S(2)}) copy-start(s32[256]{0:T(256)} %get-tuple-element.312) | copy-start | bytes 3076
  769.7 26.3 %copy-start.7 = (bf16[256,6144]{1,0:T(8,128)(2,1)S(1)}, bf16[256,6144]{1,0:T(8,128)(2,1)}, u32[]{:S(2)}) copy-start(bf16[256,6144]{1,0:T(8,128)(2,1)} %get-tuple-element.485) | copy-start | bytes 9437188 | tf_op jit(solution)/shard_map/while
  799.2 26.3 %copy-start.7 = (bf16[256,6144]{1,0:T(8,128)(2,1)S(1)}, bf16[256,6144]{1,0:T(8,128)(2,1)}, u32[]{:S(2)}) copy-start(bf16[256,6144]{1,0:T(8,128)(2,1)} %get-tuple-element.485) | copy-start | bytes 9437188 | tf_op jit(solution)/shard_map/while
  828.7 316.4 %all-reduce.2.cloned.1.call-start = ((), (), s32[]{:S(2)}) async-start(), calls=%async_computation.6 | async-start | bytes 10240000 | tf_op jit(solution)/shard_map/psum | solution.py:99
  862.5 166.7 %copy-start.5 = (f32[1024,256]{1,0:T(8,128)S(1)}, f32[1024,256]{1,0:T(8,128)}, u32[]{:S(2)}) copy-start(f32[1024,256]{1,0:T(8,128)} %reduce-scatter.6.cloned.1.call-done) | copy-start | bytes 3145732
  862.5 166.7 %copy-start.12 = (s32[256]{0:T(256)S(1)}, s32[256]{0:T(256)}, u32[]{:S(2)}) copy-start(s32[256]{0:T(256)} %get-tuple-element.308) | copy-start | bytes 3076
  (13 other events, 138.2 us)
Sparse Core Ops, SparseCore 0:
  336.9 194.5 reduce-scatter.5
  668.1 33.1 reduce-scatter.7
  828.8 29.9 reduce-scatter.3
  1046.0 99.0 all-reduce.1
where the time goes:
time: 1170 us; the launch traced here: 1160 us
  waiting for transfers between devices  545 us (47%)
  other arithmetic  407 us (35%)
  local copies, waits for them, and re-layouts  131 us (11%)
  matrix products  51.9 us (4%)
  between operations  13.9 us (1%)
    ppermute x4, waiting for transfers between devices, shifted(): return lax.ppermute(block, axis, route)  411 us
    another operation x15, other arithmetic  353 us
    psum x1, waiting for transfers between devices, per_device(): local_stack = lax.psum(local_stack, 'seg')  99.2 us
    gather x3, local copies, waits for them, and re-layouts, per_device(): first = jnp.take(own_block, first_index, axis=0).astype(jnp.float32)  49.2 us
    reduce_scatter x3, waiting for transfers between devices, per_device(): lax.psum_scatter(lax.map(one_block, offsets).reshape(lax.axis_size('lag')...  34.1 us
    gather x2, local copies, waits for them, and re-layouts, per_device(): second = jnp.take(partner_block, second_index, axis=0).astype(jnp.float32)  33.4 us
    dot_general x5, matrix products, bin_rows(): lax.dot_general(selector, corr, (((1,), (1,)), ((), ())), precision=lax.P...  26.8 us
    dot_general x12, matrix products, one_block(): lax.dot_general(table, cross, (((1,), (1,)), ((), ())), preferred_element...  25.1 us
  transfers between devices with their start and end apart: 8, of which 6 were waited for; matrix products, arithmetic and copies ran while one was open for 49% of the time, Pallas kernels for 0%

commit v1 on v0

v1 whole, which is shorter than its diff:
```python
import math

import jax
import jax.numpy as jnp
from jax import lax
from jax.sharding import PartitionSpec as P

FREQ = 6144
LAGS = 2048
ROUNDS = 3
BINS = 2
FINE = 32
BF16 = jnp.bfloat16


def shifted(block, axis, distance):
    devices = range(lax.axis_size(axis))
    route = [((i - distance) % len(devices), i) for i in devices]
    return lax.ppermute(block, axis, route)


def contract_last(a, b, out_type=jnp.float32):
    return lax.dot_general(a, b, (((1,), (1,)), ((), ())), preferred_element_type=out_type)


def pick_rows(planes, index):
    ids = jnp.arange(planes.shape[0], dtype=jnp.int32)
    hot = (index[:, None] == ids[None, :]).astype(BF16)
    return lax.dot_general(hot, planes, (((1,), (0,)), ((), ())), preferred_element_type=BF16)


def cross_spectra(first, second):
    half = first.shape[1] // 2
    a, b = first.astype(jnp.float32), second.astype(jnp.float32)
    ar, ai, br, bi = a[:, :half], a[:, half:], b[:, :half], b[:, half:]
    return jnp.concatenate([ar * br + ai * bi, ai * br - ar * bi], axis=1).astype(BF16)


def make_table(freq_index):
    def small(taus):
        phase = jnp.mod(taus[:, None] * freq_index[None, :], 2 * FREQ)
        angle = phase.astype(jnp.float32) * (math.pi / FREQ)
        return jnp.cos(angle), jnp.sin(angle)

    coarse = small(jnp.arange(LAGS // FINE, dtype=jnp.int32) * FINE - LAGS // 2)
    fine = small(jnp.arange(FINE, dtype=jnp.int32))
    (ca, sa), (cb, sb) = lax.optimization_barrier((coarse, fine))
    ca, sa, cb, sb = ca[:, None], sa[:, None], cb[None], sb[None]
    cos = (ca * cb - sa * sb).astype(BF16).reshape(LAGS, -1)
    neg_sin = (-(sa * cb + ca * sb)).astype(BF16).reshape(LAGS, -1)
    return jnp.concatenate([cos, neg_sin], axis=1)


def selector(rows, active, total_rows):
    ids = jnp.arange(total_rows, dtype=jnp.int32)[:, None]
    return ((ids == rows[None, :]) & active[None, :]).astype(BF16)


def per_device(spectra, pair_local, pair_partner, pair_bin, pair_owner, pair_count):
    blocks = lax.axis_size("chan")
    me = lax.axis_index("chan")
    lag_index = lax.axis_index("lag")
    own = spectra[0]
    block_chans, _, half_freq = own.shape
    half_lags = LAGS // lax.axis_size("lag")
    total_rows = block_chans * BINS
    slots = pair_local.shape[2]
    half = slots // 2
    slot_ids = jnp.arange(slots, dtype=jnp.int32)
    planes = jnp.concatenate([own[:, 0], own[:, 1]], axis=1)

    sent = {}
    for r in range(1, ROUNDS):
        before = lax.rem(me - r + blocks, blocks)
        to_first = pick_rows(planes, pair_partner[before, r, 0::2])
        to_partner = pick_rows(planes, pair_local[me, r, 1::2])
        cuts = [(0, half)] if r == 1 else [(0, half // 2), (half // 2, half)]
        for lo, hi in cuts:
            sent[r, lo, hi] = (
                shifted(to_first[lo:hi], "chan", -r),
                shifted(to_partner[lo:hi], "chan", r),
            )

    freq_index = lag_index * half_freq + jnp.arange(half_freq, dtype=jnp.int32) + 1
    table = make_table(freq_index)
    corr_scale = FREQ ** (-0.5)

    def correlate(cross):
        part = (contract_last(table, cross) * corr_scale).astype(BF16)
        return lax.psum_scatter(part, ("lag", "seg"), scatter_dimension=0, tiled=True)

    def chosen(b, r, step, lo, hi, owner):
        def cut(values):
            return values[step::2][lo:hi]

        channel = pair_local if owner == 0 else pair_partner
        rows = cut(channel[b, r]) * BINS + cut(pair_bin[b, r])
        live = cut(slot_ids) < pair_count[b, r]
        return rows, live & (cut(pair_owner[b, r]) == owner)

    pieces = []
    own_pairs = cross_spectra(
        pick_rows(planes, pair_local[me, 0]), pick_rows(planes, pair_partner[me, 0])
    )
    rows0 = jnp.where(pair_owner[me, 0] == 0, pair_local[me, 0], pair_partner[me, 0])
    pieces.append(
        (correlate(own_pairs), [(rows0 * BINS + pair_bin[me, 0], slot_ids < pair_count[me, 0])])
    )
    for (r, lo, hi), (second, first) in sent.items():
        before = lax.rem(me - r + blocks, blocks)
        here = hi - lo
        crosses = jnp.concatenate(
            [
                cross_spectra(pick_rows(planes, pair_local[me, r, 0::2][lo:hi]), second),
                cross_spectra(first, pick_rows(planes, pair_partner[before, r, 1::2][lo:hi])),
            ],
            axis=0,
        )
        corr = correlate(crosses)
        from_after = shifted(corr[:, here:], "chan", -r)
        from_before = shifted(corr[:, :here], "chan", r)
        pieces.append(
            (
                jnp.concatenate([corr, from_after, from_before], axis=1),
                [
                    chosen(me, r, 0, lo, hi, 0),
                    chosen(before, r, 1, lo, hi, 1),
                    chosen(me, r, 1, lo, hi, 0),
                    chosen(before, r, 0, lo, hi, 1),
                ],
            )
        )

    def stacked(some):
        corr = jnp.concatenate([piece for piece, _ in some], axis=1)
        corr = lax.all_gather(corr, "seg", axis=0, tiled=True)
        rows = jnp.concatenate([rows for _, picks in some for rows, _ in picks])
        active = jnp.concatenate([live for _, picks in some for _, live in picks])
        return contract_last(selector(rows, active, total_rows), corr)

    result = stacked(pieces[:-1]) + stacked(pieces[-1:])
    return result.reshape(block_chans, BINS, half_lags)


def solution(mesh):
    return jax.shard_map(
        per_device,
        mesh=mesh,
        in_specs=(P("seg", "chan", None, "lag"), P(), P(), P(), P(), P()),
        out_specs=P("chan", None, "lag"),
        check_vma=False,
    )
```

time: 1170 us -> 421 us (0.36)
  waiting for transfers between devices: 545 us -> 166 us
  other arithmetic: 407 us -> 40.9 us
  local copies, waits for them, and re-layouts: 131 us -> 52.9 us
  matrix products: 51.9 us -> 109 us
    another operation x15 -> x7, other arithmetic: 353 us -> 5.52 us
    ppermute x4 -> x12, waiting for transfers between devices: 411 us -> 113 us  [shifted(): return lax.ppermute(block, axis, route)]
    psum x1 -> x0, waiting for transfers between devices: 99.2 us -> none  [per_device(): local_stack = lax.psum(local_stack, 'seg')]
    gather x6 -> x8, local copies, waits for them, and re-layouts: 99.1 us -> 13.6 us  [the longest x2 3.41 us: per_device(): to_first = pick_rows(planes, pair_partner[before, r, 0::2])]
    dot_general x17 -> x18, matrix products: 51.9 us -> 109 us  [the longest x6 60.5 us: contract_last(): lax.dot_general(a, b, (((1,), (1,)), ((), ())), preferred_element_type=ou...]
    reduce_scatter x3 -> x4, waiting for transfers between devices: 34.1 us -> 50.9 us  [correlate(): lax.psum_scatter(part, ('lag', 'seg'), scatter_dimension=0, tiled=True)]
    convert_element_type x6 -> x7, other arithmetic: 34.6 us -> 23.2 us  [the longest x1 14.7 us: make_table(): cos = (ca * cb - sa * sb).astype(BF16).reshape(LAGS, -1)]
  transfers between devices with their start and end apart: 8 -> 17, of which waited for: 6 -> 8; matrix products, arithmetic and copies ran while one was open for 49% -> 40% of each run, Pallas kernels for 0% -> 0%
where the time goes in v1:
time: 421 us; the launch traced here: 413 us
  waiting for transfers between devices  166 us (39%)
  matrix products  109 us (26%)
  local copies, waits for them, and re-layouts  52.9 us (13%)
  other arithmetic  40.9 us (10%)
  starting transfers between devices  19.6 us (5%)
  between operations  13.9 us (3%)
  blocking collectives  10.7 us (3%)
    ppermute x12, waiting for transfers between devices, shifted(): return lax.ppermute(block, axis, route)  113 us
    dot_general x6, matrix products, contract_last(): lax.dot_general(a, b, (((1,), (1,)), ((), ())), preferred_element_type=ou...  60.5 us
    reduce_scatter x4, waiting for transfers between devices, correlate(): lax.psum_scatter(part, ('lag', 'seg'), scatter_dimension=0, tiled=True)  50.9 us
    dot_general x12, matrix products, pick_rows(): lax.dot_general(hot, planes, (((1,), (0,)), ((), ())), preferred_element_...  48.6 us
    ppermute x12, starting transfers between devices, shifted(): return lax.ppermute(block, axis, route)  19.3 us
    convert_element_type x1, other arithmetic, make_table(): cos = (ca * cb - sa * sb).astype(BF16).reshape(LAGS, -1)  14.7 us
    all_gather x1, blocking collectives, stacked(): corr = lax.all_gather(corr, 'seg', axis=0, tiled=True)  10.7 us
    unnamed x31, local copies, waits for them, and re-layouts  9.59 us
  transfers between devices with their start and end apart: 17, of which 8 were waited for; matrix products, arithmetic and copies ran while one was open for 40% of the time, Pallas kernels for 0%

profile of v1, /device:TPU:0, one launch (start us, length us, event | category | flops | bytes accessed | tf_op | source)
XLA Modules:
  0.0 413.4 jit_solution(9490124610198681511)
XLA Ops:
  6.5 8.6 %copy.10 = bf16[1,625,2,3072]{3,1,2,0:T(8,128)(2,1)} copy(bf16[1,625,2,3072]{3,2,1,0:T(2,128)(2,1)} %param.6) | data formatting | bytes 15360000 | tf_op args[0]
  15.1 5.7 %slice_bitcast_fusion.1 = (bf16[625,3072]{1,0:T(8,128)(2,1)}, bf16[625,3072]{1,0:T(8,128)(2,1)}) fusion(bf16[625,2,3072]{2,0,1:T(8,128)(2,1)} %bitcast.47), kind=kLoop, calls=%fused_computation.26 | loop fusion | bytes 15360000 | tf_op jit(solution)/shard_map/squeeze | solution.py:70
  22.5 4.8 %fusion.71 = bf16[128,6144]{1,0:T(8,128)(2,1)S(1)} fusion(s32[128]{0:T(128)S(1)} %gather_fusion.5, bf16[625,3072]{1,0:T(8,128)(2,1)} %get-tuple-element.16, bf16[625,3072]{1,0:T(8,128)(2,1)} %get-tuple-element.15), kind=kOutput, calls=%fused_computation.112 | convolution fusion | flops 998480000 | bytes 9253376 | tf_op jit(solution)/shard_map/dot_general | solution.py:29
  28.6 4.0 collective-permute-start.4
  34.4 4.8 %fusion.72 = bf16[128,6144]{1,0:T(8,128)(2,1)S(1)} fusion(s32[128]{0:T(128)S(1)} %gather_fusion.6, bf16[625,3072]{1,0:T(8,128)(2,1)} %get-tuple-element.16, bf16[625,3072]{1,0:T(8,128)(2,1)} %get-tuple-element.15), kind=kOutput, calls=%fused_computation.113 | convolution fusion | flops 998480000 | bytes 9253376 | tf_op jit(solution)/shard_map/dot_general | solution.py:29
  45.2 6.0 %fusion.70 = bf16[128,6144]{1,0:T(8,128)(2,1)} fusion(s32[128]{0:T(128)S(1)} %gather_fusion.2, bf16[625,3072]{1,0:T(8,128)(2,1)} %get-tuple-element.16, bf16[625,3072]{1,0:T(8,128)(2,1)} %get-tuple-element.15), kind=kOutput, calls=%fused_computation.111 | convolution fusion | flops 998480000 | bytes 9253376 | tf_op jit(solution)/shard_map/dot_general | solution.py:29
  68.7 6.2 %fusion.69 = bf16[128,6144]{1,0:T(8,128)(2,1)} fusion(s32[128]{0:T(128)S(1)} %gather_fusion.1, bf16[625,3072]{1,0:T(8,128)(2,1)} %get-tuple-element.16, bf16[625,3072]{1,0:T(8,128)(2,1)} %get-tuple-element.15), kind=kOutput, calls=%fused_computation.110 | convolution fusion | flops 998480000 | bytes 9253376 | tf_op jit(solution)/shard_map/dot_general | solution.py:29
  74.9 5.0 %convolution_convert_fusion.3 = f32[128,6144]{1,0:T(8,128)} fusion(s32[128]{0:T(128)S(1)} %gather_fusion, bf16[625,3072]{1,0:T(8,128)(2,1)S(1)} %copy-done.4, bf16[625,3072]{1,0:T(8,128)(2,1)S(1)} %copy-done.2), kind=kOutput, calls=%fused_computation.16 | convolution fusion | flops 999266432 | bytes 10826240 | tf_op jit(solution)/shard_map/dot_general | solution.py:29
  79.9 5.2 %convolution_convert_fusion.2 = f32[128,6144]{1,0:T(8,128)} fusion(s32[128]{0:T(128)S(1)} %gather_fusion.3, bf16[625,3072]{1,0:T(8,128)(2,1)S(1)} %copy-done.4, bf16[625,3072]{1,0:T(8,128)(2,1)S(1)} %copy-done.2), kind=kOutput, calls=%fused_computation.15 | convolution fusion | flops 999266432 | bytes 10826240 | tf_op jit(solution)/shard_map/dot_general | solution.py:29
  91.0 3.4 add_convert_fusion
  94.4 14.7 %subtract_convert_fusion = (bf16[64,32,3072]{2,1,0:T(8,128)(2,1)}, bf16[64,32,3072]{2,1,0:T(8,128)(2,1)}) fusion(f32[32,3072]{1,0:T(8,128)S(1)} %get-tuple-element.12, f32[64,3072]{1,0:T(8,128)S(1)} %get-tuple-element.11, f32[32,3072]{1,0:T(8,128)} %get-tuple-element.10, f32[64,3072]{1,0:T(8,128)S(1)} %get-tuple-element.9), kind=kLoop, calls=%fused_computation.10 | loop fusion | flops 56623104 | bytes 27525120 | tf_op jit(solution)/shard_map/convert_element_type | solution.py:49
  112.8 39.6 %collective-permute-done.4 = bf16[64,6144]{1,0:T(8,128)(2,1)} collective-permute-done((bf16[64,6144]{1,0:T(8,128)(2,1)}, bf16[64,6144]{1,0:T(8,128)(2,1)}, u32[]{:S(2)}, u32[]{:S(2)}) %collective-permute-start.4) | collective-permute-done | bytes 786464 | tf_op jit(solution)/shard_map/ppermute | solution.py:19
  154.3 31.9 %collective-permute-done.5 = bf16[64,6144]{1,0:T(8,128)(2,1)} collective-permute-done((bf16[64,6144]{1,0:T(8,128)(2,1)}, bf16[64,6144]{1,0:T(8,128)(2,1)}, u32[]{:S(2)}, u32[]{:S(2)}) %collective-permute-start.5) | collective-permute-done | bytes 786464 | tf_op jit(solution)/shard_map/ppermute | solution.py:19
  187.7 12.3 %fusion.32 = bf16[2048,128]{1,0:T(8,128)(2,1)} fusion(bf16[64,3072]{1,0:T(8,128)(2,1)S(1)} %get-tuple-element.24, bf16[64,3072]{1,0:T(8,128)(2,1)S(1)} %get-tuple-element.23, bf16[64,3072]{1,0:T(8,128)(2,1)S(1)} %get-tuple-element.22, bf16[64,3072]{1,0:T(8,128)(2,1)S(1)} %get-tuple-element.21, bf16[2048,3072]{1,0:T(8,128)(2,1)} %bitcast.52, ...), kind=kOutput, calls=%fused_computation.49 | convolution fusion | flops 3278372864 | bytes 27262976 | tf_op jit(solution)/shard_map/dot_general | solution.py:23
  200.1 35.8 %collective-permute-done = bf16[128,6144]{1,0:T(8,128)(2,1)} collective-permute-done((bf16[128,6144]{1,0:T(8,128)(2,1)}, bf16[128,6144]{1,0:T(8,128)(2,1)}, u32[]{:S(2)}, u32[]{:S(2)}) %collective-permute-start) | collective-permute-done | bytes 1572896 | tf_op jit(solution)/shard_map/ppermute | solution.py:19
  241.3 12.7 %fusion.24 = bf16[2048,256]{1,0:T(8,128)(2,1)} fusion(bf16[128,3072]{1,0:T(8,128)(2,1)S(1)} %get-tuple-element.20, bf16[128,3072]{1,0:T(8,128)(2,1)S(1)} %get-tuple-element.19, bf16[128,3072]{1,0:T(8,128)(2,1)S(1)} %get-tuple-element.18, bf16[128,3072]{1,0:T(8,128)(2,1)S(1)} %get-tuple-element.17, bf16[2048,3072]{1,0:T(8,128)(2,1)} %bitcast.53, ...), kind=kOutput, calls=%fused_computation.43 | convolution fusion | flops 6506414080 | bytes 29360128 | tf_op jit(solution)/shard_map/dot_general | solution.py:23
  254.1 12.9 %fusion.27 = bf16[2048,256]{1,0:T(8,128)(2,1)} fusion(bf16[256,3072]{1,0:T(8,128)(2,1)S(1)} %copy-done.9, bf16[256,3072]{1,0:T(8,128)(2,1)S(1)} %copy-done.8, bf16[2048,3072]{1,0:T(8,128)(2,1)} %bitcast.54, bf16[2048,3072]{1,0:T(8,128)(2,1)} %bitcast.50), kind=kOutput, calls=%fused_computation.44 | convolution fusion | flops 6500122624 | bytes 29360128 | tf_op jit(solution)/shard_map/dot_general | solution.py:23
  267.3 5.0 %convolution_convert_fusion.5 = f32[64,6144]{1,0:T(8,128)S(1)} fusion(s32[64]{0:T(128)S(1)} %get-tuple-element.90, bf16[625,3072]{1,0:T(8,128)(2,1)} %get-tuple-element.16, bf16[625,3072]{1,0:T(8,128)(2,1)} %get-tuple-element.15), kind=kOutput, calls=%fused_computation.18 | convolution fusion | flops 507313216 | bytes 9253120 | tf_op jit(solution)/shard_map/dot_general | solution.py:29
  277.8 12.4 %fusion.33 = bf16[2048,128]{1,0:T(8,128)(2,1)} fusion(bf16[64,3072]{1,0:T(8,128)(2,1)S(1)} %get-tuple-element.28, bf16[64,3072]{1,0:T(8,128)(2,1)S(1)} %get-tuple-element.27, bf16[64,3072]{1,0:T(8,128)(2,1)S(1)} %get-tuple-element.26, bf16[64,3072]{1,0:T(8,128)(2,1)S(1)} %get-tuple-element.25, bf16[2048,3072]{1,0:T(8,128)(2,1)} %bitcast.55, ...), kind=kOutput, calls=%fused_computation.50 | convolution fusion | flops 3278372864 | bytes 27262976 | tf_op jit(solution)/shard_map/dot_general | solution.py:23
  303.5 24.7 %reduce-scatter.5.cloned.1.call-done = bf16[256,256]{1,0:T(8,128)(2,1)} async-done(((bf16[2048,256]{1,0:T(8,128)(2,1)}), bf16[256,256]{1,0:T(8,128)(2,1)}) %reduce-scatter.5.cloned.1.call-update) | async-done | bytes 131088 | tf_op jit(solution)/shard_map/reduce_scatter | solution.py:90
  339.3 26.2 %reduce-scatter.11.cloned.1.call-done = bf16[256,128]{1,0:T(8,128)(2,1)} async-done(((bf16[2048,128]{1,0:T(8,128)(2,1)}), bf16[256,128]{1,0:T(8,128)(2,1)}) %reduce-scatter.11.cloned.1.call-update) | async-done | bytes 65552 | tf_op jit(solution)/shard_map/reduce_scatter | solution.py:90
  376.2 10.7 %all_gather.7 = bf16[1024,256]{1,0:T(8,128)(2,1)S(1)} all-gather(bf16[256,256]{1,0:T(8,128)(2,1)S(1)} %pad_maximum_fusion.2), channel_id=1, replica_groups=mesh['chan'=4,'seg'=4,'lag'=2] {'seg'}, dimensions={0}, use_global_device_ids=true | all-gather | bytes 655360 | tf_op jit(solution)/shard_map/all_gather | solution.py:136
  392.4 7.0 %fusion.3 = f32[1250,1024]{1,0:T(8,128)} fusion(f32[1250,1024]{1,0:T(8,128)} %fusion.49, bf16[1024,1024]{1,0:T(8,128)(2,1)} %all-gather.2.cloned.1.call-done, s32[1024]{0:T(1024)S(1)} %concatenate.87, pred[1024]{0:T(1024)(128)(4,1)S(1)} %concatenate.88), kind=kOutput, calls=%fused_computation.24 | convolution fusion | flops 2625280000 | bytes 12342272 | tf_op jit(solution)/shard_map/dot_general | solution.py:23
  399.3 7.3 %reshape.65 = f32[625,2,1024]{2,1,0:T(2,128)} reshape(f32[1250,1024]{1,0:T(8,128)} %fusion.3) | data formatting | bytes 10240000 | tf_op jit(solution)/shard_map/reshape | solution.py:142
  (153 shorter events, 92.4 us)
Async XLA Ops:
  6.5 283.8 %reduce-scatter.9.cloned.1.call-start = ((), (), s32[]{:S(2)}) async-start(), calls=%async_computation.6 | async-start | bytes 589824 | tf_op jit(solution)/shard_map/reduce_scatter | solution.py:90
  28.6 123.8 %collective-permute-start.4 = (bf16[64,6144]{1,0:T(8,128)(2,1)}, bf16[64,6144]{1,0:T(8,128)(2,1)}, u32[]{:S(2)}, u32[]{:S(2)}) collective-permute-start(bf16[64,6144]{1,0:T(8,128)(2,1)} %get-tuple-element.31), channel_id=1, source_target_pairs={{16,0},{24,8},{0,16},{8,24},{17,1},{25,9},{1,17},{9,25},{18,2},{26... | collective-permute-start | bytes 2359304 | tf_op jit(solution)/shard_map/ppermute | solution.py:19
  32.7 242.1 %collective-permute-start.8 = (bf16[64,6144]{1,0:T(8,128)(2,1)}, bf16[64,6144]{1,0:T(8,128)(2,1)}, u32[]{:S(2)}, u32[]{:S(2)}) collective-permute-start(bf16[64,6144]{1,0:T(8,128)(2,1)} %get-tuple-element.32), channel_id=1, source_target_pairs={{16,0},{24,8},{0,16},{8,24},{17,1},{25,9},{1,17},{9,25},{18,2},{26... | collective-permute-start | bytes 2359304 | tf_op jit(solution)/shard_map/ppermute | solution.py:19
  40.5 145.7 %collective-permute-start.5 = (bf16[64,6144]{1,0:T(8,128)(2,1)}, bf16[64,6144]{1,0:T(8,128)(2,1)}, u32[]{:S(2)}, u32[]{:S(2)}) collective-permute-start(bf16[64,6144]{1,0:T(8,128)(2,1)} %get-tuple-element.33), channel_id=1, source_target_pairs={{16,0},{24,8},{0,16},{8,24},{17,1},{25,9},{1,17},{9,25},{18,2},{26... | collective-permute-start | bytes 2359304 | tf_op jit(solution)/shard_map/ppermute | solution.py:19
  43.4 232.8 %collective-permute-start.9 = (bf16[64,6144]{1,0:T(8,128)(2,1)}, bf16[64,6144]{1,0:T(8,128)(2,1)}, u32[]{:S(2)}, u32[]{:S(2)}) collective-permute-start(bf16[64,6144]{1,0:T(8,128)(2,1)} %get-tuple-element.34), channel_id=1, source_target_pairs={{16,0},{24,8},{0,16},{8,24},{17,1},{25,9},{1,17},{9,25},{18,2},{26... | collective-permute-start | bytes 2359304 | tf_op jit(solution)/shard_map/ppermute | solution.py:19
  51.2 187.0 %collective-permute-start.1 = (bf16[128,6144]{1,0:T(8,128)(2,1)}, bf16[128,6144]{1,0:T(8,128)(2,1)}, u32[]{:S(2)}, u32[]{:S(2)}) collective-permute-start(bf16[128,6144]{1,0:T(8,128)(2,1)} %fusion.70), channel_id=1, source_target_pairs={{24,0},{0,8},{8,16},{16,24},{25,1},{1,9},{9,17},{17,25},{26,2},{2,... | collective-permute-start | bytes 4718600 | tf_op jit(solution)/shard_map/ppermute | solution.py:19
  152.5 83.4 %collective-permute-start = (bf16[128,6144]{1,0:T(8,128)(2,1)}, bf16[128,6144]{1,0:T(8,128)(2,1)}, u32[]{:S(2)}, u32[]{:S(2)}) collective-permute-start(bf16[128,6144]{1,0:T(8,128)(2,1)} %fusion.69), channel_id=1, source_target_pairs={{8,0},{16,8},{24,16},{0,24},{9,1},{17,9},{25,17},{1,25},{10,2},{18... | collective-permute-start | bytes 4718600 | tf_op jit(solution)/shard_map/ppermute | solution.py:19
  200.0 37.6 %copy-start.7 = (f32[128,6144]{1,0:T(8,128)S(1)}, f32[128,6144]{1,0:T(8,128)}, u32[]{:S(2)}) copy-start(f32[128,6144]{1,0:T(8,128)} %convolution_convert_fusion.3) | copy-start | bytes 9437188
  200.1 94.2 %reduce-scatter.7.cloned.1.call-start = ((), (), s32[]{:S(2)}) async-start(), calls=%async_computation.5 | async-start | bytes 1179648 | tf_op jit(solution)/shard_map/reduce_scatter | solution.py:90
  241.3 12.8 %copy-start.8 = (bf16[256,3072]{1,0:T(8,128)(2,1)S(1)}, bf16[256,3072]{1,0:T(8,128)(2,1)}, u32[]{:S(2)}) copy-start(bf16[256,3072]{1,0:T(8,128)(2,1)} %get-tuple-element.13) | copy-start | bytes 4718596
  254.1 74.1 %reduce-scatter.5.cloned.1.call-start = ((), (), s32[]{:S(2)}) async-start(), calls=%async_computation.4 | async-start | bytes 1179648 | tf_op jit(solution)/shard_map/reduce_scatter | solution.py:90
  267.1 98.5 %reduce-scatter.11.cloned.1.call-start = ((), (), s32[]{:S(2)}) async-start(), calls=%async_computation.8 | async-start | bytes 589824 | tf_op jit(solution)/shard_map/reduce_scatter | solution.py:90
  277.7 22.1 %copy-start.14 = (s32[1,1,256]{2,0,1:T(1,128)S(1)}, s32[1,1,256]{2,0,1:T(1,128)}, u32[]{:S(2)}) copy-start(s32[1,1,256]{2,0,1:T(1,128)} %get-tuple-element.56) | copy-start | bytes 3076
  277.7 22.6 %copy-start.13 = (s32[1,1,256]{2,0,1:T(1,128)S(1)}, s32[1,1,256]{2,0,1:T(1,128)}, u32[]{:S(2)}) copy-start(s32[1,1,256]{2,0,1:T(1,128)} %get-tuple-element.55) | copy-start | bytes 3076
  277.7 23.0 %copy-start.12 = (s32[1,1,256]{2,0,1:T(1,128)S(1)}, s32[1,1,256]{2,0,1:T(1,128)}, u32[]{:S(2)}) copy-start(s32[1,1,256]{2,0,1:T(1,128)} %get-tuple-element.48) | copy-start | bytes 3076
  277.7 23.5 %copy-start.11 = (s32[1,1,256]{2,0,1:T(1,128)S(1)}, s32[1,1,256]{2,0,1:T(1,128)}, u32[]{:S(2)}) copy-start(s32[1,1,256]{2,0,1:T(1,128)} %get-tuple-element.47) | copy-start | bytes 3076
  277.8 56.0 %copy-start.10 = (s32[4,3]{1,0:T(4,128)S(1)}, s32[4,3]{1,0:T(4,128)}, u32[]{:S(2)}) copy-start(s32[4,3]{1,0:T(4,128)} %param.11) | copy-start | bytes 148
  290.2 102.1 %all-gather.2.cloned.1.call-start = ((), (), s32[]{:S(2)}) async-start(), calls=%async_computation.7 | async-start | bytes 2621440 | tf_op jit(solution)/shard_map/all_gather | solution.py:136
  291.3 36.8 %collective-permute-start.7 = (bf16[256,64]{1,0:T(8,128)(2,1)S(1)}, bf16[256,64]{1,0:T(8,128)(2,1)S(1)}, u32[]{:S(2)}, u32[]{:S(2)}) collective-permute-start(bf16[256,64]{1,0:T(8,128)(2,1)S(1)} %get-tuple-element.37), channel_id=1, source_target_pairs={{16,0},{24,8},{0,16},{8,24},{17,1},{25,9},{1,17},{9,25},{18,2},{26... | collective-permute-start | bytes 98312 | tf_op jit(solution)/shard_map/ppermute | solution.py:19
  291.4 36.7 %collective-permute-start.6 = (bf16[256,64]{1,0:T(8,128)(2,1)S(1)}, bf16[256,64]{1,0:T(8,128)(2,1)S(1)}, u32[]{:S(2)}, u32[]{:S(2)}) collective-permute-start(bf16[256,64]{1,0:T(8,128)(2,1)S(1)} %get-tuple-element.38), channel_id=1, source_target_pairs={{16,0},{24,8},{0,16},{8,24},{17,1},{25,9},{1,17},{9,25},{18,2},{26... | collective-permute-start | bytes 98312 | tf_op jit(solution)/shard_map/ppermute | solution.py:19
  295.2 32.9 %collective-permute-start.3 = (bf16[256,128]{1,0:T(8,128)(2,1)S(1)}, bf16[256,128]{1,0:T(8,128)(2,1)S(1)}, u32[]{:S(2)}, u32[]{:S(2)}) collective-permute-start(bf16[256,128]{1,0:T(8,128)(2,1)S(1)} %get-tuple-element.35), channel_id=1, source_target_pairs={{24,0},{0,8},{8,16},{16,24},{25,1},{1,9},{9,17},{17,25},{26,2},{2,... | collective-permute-start | bytes 196616 | tf_op jit(solution)/shard_map/ppermute | solution.py:19
  295.8 32.3 %collective-permute-start.2 = (bf16[256,128]{1,0:T(8,128)(2,1)S(1)}, bf16[256,128]{1,0:T(8,128)(2,1)S(1)}, u32[]{:S(2)}, u32[]{:S(2)}) collective-permute-start(bf16[256,128]{1,0:T(8,128)(2,1)S(1)} %get-tuple-element.36), channel_id=1, source_target_pairs={{8,0},{16,8},{24,16},{0,24},{9,1},{17,9},{25,17},{1,25},{10,2},{18... | collective-permute-start | bytes 196616 | tf_op jit(solution)/shard_map/ppermute | solution.py:19
  366.6 5.5 %collective-permute-start.10 = (bf16[256,64]{1,0:T(8,128)(2,1)S(1)}, bf16[256,64]{1,0:T(8,128)(2,1)S(1)}, u32[]{:S(2)}, u32[]{:S(2)}) collective-permute-start(bf16[256,64]{1,0:T(8,128)(2,1)S(1)} %get-tuple-element.39), channel_id=1, source_target_pairs={{16,0},{24,8},{0,16},{8,24},{17,1},{25,9},{1,17},{9,25},{18,2},{26... | collective-permute-start | bytes 98312 | tf_op jit(solution)/shard_map/ppermute | solution.py:19
  369.0 6.3 %collective-permute-start.11 = (bf16[256,64]{1,0:T(8,128)(2,1)S(1)}, bf16[256,64]{1,0:T(8,128)(2,1)S(1)}, u32[]{:S(2)}, u32[]{:S(2)}) collective-permute-start(bf16[256,64]{1,0:T(8,128)(2,1)S(1)} %get-tuple-element.40), channel_id=1, source_target_pairs={{16,0},{24,8},{0,16},{8,24},{17,1},{25,9},{1,17},{9,25},{18,2},{26... | collective-permute-start | bytes 98312 | tf_op jit(solution)/shard_map/ppermute | solution.py:19
  (8 other events, 54.1 us)
Sparse Core Ops, SparseCore 0:
  200.2 32.6 reduce-scatter.8
  254.2 34.3 reduce-scatter.6
  292.1 36.0 reduce-scatter.4
  331.4 34.1 reduce-scatter.10
  367.0 25.3 all-gather.1
